TPU v7x, 256 devices: a whole 4x4x8 slice. The times are simulated.
256 devices in a mesh: vert: 128 (over z, y, x), qcol: 2 (over core).
Axes of the slice: x: 4, y: 4, z: 8, core: 2. Of those that a mesh axis runs over, the one named last changes fastest.
Arguments:
- descriptors: bfloat16 [262144, 2048], P('vert'), may hold values from -0.8984375 to 0.8984375
- queries: bfloat16 [512, 2048], P('qcol', 'vert'), may hold values from -0.8984375 to 0.8984375
- tiles: bfloat16 [6144, 128, 128], P('vert'), may hold values from 0 to 1, as said below
- tile_cols: int32 [128, 3, 16], replicated, may hold values from 0 to 15, as said below
- part_size: int32 [128], replicated, may hold values from 1024 to 2048, as said below
Outputs:
- ranking: float32 [262144, 512], P('vert', 'qcol')
- residual: float32 [262144, 512], P('vert', 'qcol')
Inputs may be any that keep to these rules, and one draw needn't show every extreme that they name: For each part d and slot j, tile_cols[d, j, :] is a permutation of 0 to 15. `part_size`: some part has exactly 2048 live vertices and some exactly 1024. tiles are sparse and nonnegative; every row and every column of B sums to at most 1.01.
All inputs are finite; a program needn't handle non-finite values.
Results may differ from a plain program's by a relative error of at most 0.0003.
Values may be sent and summed in bfloat16 or wider, within the bound.
A program may use at most 128 MiB of HBM per device.

v0:
```python
import jax
import jax.numpy as jnp
from jax import lax
from jax.sharding import PartitionSpec as P

ITERS = 2


def padded(block, sides, width):
    for axis, dim in sides:
        count = lax.axis_size(axis)
        forward = [(i, i + 1) for i in range(count - 1)]
        forward.append((count - 1, 0))
        backward = [(target, source) for source, target in forward]
        low = lax.ppermute(
            lax.slice_in_dim(block, block.shape[dim] - width, None, axis=dim), axis, forward
        )
        high = lax.ppermute(lax.slice_in_dim(block, 0, width, axis=dim), axis, backward)
        block = jnp.concatenate([low, block, high], axis=dim)
    return block


def shifted(x, axis, by):
    peers = lax.axis_size(axis)
    return lax.ppermute(x, axis, [(i, (i + by) % peers) for i in range(peers)])


def transposed(blocks_slot, rows3, cols_row):
    moved = jnp.einsum("rba,rbq->raq", blocks_slot, rows3, precision=lax.Precision.HIGHEST)
    return moved[jnp.argsort(cols_row)]


def body(descriptors, queries, tiles, tile_cols, part_size):
    rows = descriptors.shape[0]
    qdev = queries.shape[0]
    tile = tiles.shape[1]
    rtiles = rows // tile
    slots = tiles.shape[0] // rtiles
    here = lax.axis_index("vert")
    sims = lax.dot_general(
        descriptors,
        lax.all_gather(queries, "vert", axis=1, tiled=True),
        (((1,), (1,)), ((), ())),
        preferred_element_type=jnp.float32,
    )
    live_count = lax.dynamic_index_in_dim(part_size, here, 0, keepdims=False)
    live = (lax.iota(jnp.int32, rows) < live_count).astype(jnp.float32)[:, None]
    seeds = live * jnp.maximum(sims, 0.0) ** 3
    blocks = tiles.astype(jnp.float32).reshape(slots, rtiles, tile, tile)
    own_cols = lax.dynamic_index_in_dim(tile_cols, here, 0, keepdims=False)

    def squares(values):
        return lax.psum(jnp.sum(values * values, axis=0), "vert")

    ranking = jnp.zeros_like(seeds)
    residual = seeds
    direction = seeds
    norm_now = squares(residual)
    for step in range(ITERS):
        widened = padded(direction, (("vert", 0),), rows)
        forward = jnp.zeros((rtiles, tile, qdev), jnp.float32)
        for slot in range(slots):
            source = widened[slot * rows : (slot + 1) * rows].reshape(rtiles, tile, qdev)
            picked = source[own_cols[slot]]
            forward = forward + jnp.einsum(
                "rab,rbq->raq", blocks[slot], picked, precision=lax.Precision.HIGHEST
            )
        own3 = direction.reshape(rtiles, tile, qdev)
        middle = transposed(blocks[1], own3, own_cols[1])
        toward_low = transposed(blocks[0], own3, own_cols[0])
        toward_high = transposed(blocks[slots - 1], own3, own_cols[slots - 1])
        back = middle + shifted(toward_low, "vert", -1) + shifted(toward_high, "vert", 1)
        both = (forward + back).reshape(rows, qdev)
        image = direction - 0.99 * live * (0.5 * both)
        curve = lax.psum(jnp.sum(direction * image, axis=0), "vert")
        alpha = norm_now / curve
        ranking = ranking + alpha[None, :] * direction
        residual = residual - alpha[None, :] * image
        norm_next = squares(residual)
        direction = residual + (norm_next / norm_now)[None, :] * direction
        norm_now = norm_next
    return (ranking, residual)


def solution(mesh):
    placed = (P("vert", None), P("qcol", "vert"), P("vert", None, None), P(), P())
    return jax.shard_map(
        body,
        mesh=mesh,
        in_specs=placed,
        out_specs=(P("vert", "qcol"), P("vert", "qcol")),
        check_vma=False,
    )
```

profile of v0, /device:TPU:0, one launch (start us, length us, event | category | flops | bytes accessed | tf_op | source)
XLA Modules:
  0.0 1348.9 jit_solution(10652084589290533953)
XLA Ops:
  14.6 100.5 %all-gather.2.cloned.1.call-done = bf16[256,2048]{0,1:T(8,128)(2,1)} async-done(((bf16[256,16]{0,1:T(8,128)(2,1)}), bf16[256,2048]{0,1:T(8,128)(2,1)}) %all-gather.2.cloned.1.call-update) | async-done | bytes 1048592 | tf_op jit(solution)/shard_map/all_gather | solution.py:42
  115.1 6.1 fusion
  122.6 6.1 collective-permute-start.1
  128.7 4.3 convolution_bitcast_fusion.4
  140.9 4.3 convolution_bitcast_fusion.3
  153.1 4.3 convolution_bitcast_fusion.5
  165.9 4.1 fusion.17
  170.0 5.3 collective-permute-done
  175.4 3.6 gather_fusion
  179.0 3.7 gather_fusion.2
  185.7 28.8 %collective-permute-done.2 = f32[16,128,256]{2,1,0:T(8,128)} collective-permute-done((f32[16,128,256]{2,1,0:T(8,128)}, f32[16,128,256]{2,1,0:T(8,128)}, u32[]{:S(2)}, u32[]{:S(2)}) %collective-permute-start.2) | collective-permute-done | bytes 2097184 | tf_op jit(solution)/shard_map/ppermute | solution.py:25
  215.2 5.1 bitcast_add_fusion.1
  221.7 349.4 %all-reduce = (f32[256]{0:T(256)S(1)}, f32[256]{0:T(256)S(1)}) all-reduce(f32[256]{0:T(256)S(1)} %get-tuple-element.9, f32[256]{0:T(256)S(1)} %get-tuple-element.8), channel_id=1, replica_groups=mesh['vert'=128,'qcol'=2] {'vert'}, use_global_device_ids=true, to_apply=%region_1.2 | all-reduce | flops 512 | bytes 4096 | tf_op jit(solution)/shard_map/psum | solution.py:53
  573.1 343.0 %psum.30 = f32[256]{0:T(256)S(1)} all-reduce(f32[256]{0:T(256)S(1)} %multiply_reduce_fusion.1), channel_id=1, replica_groups=mesh['vert'=128,'qcol'=2] {'vert'}, use_global_device_ids=true, to_apply=%region_8.9 | all-reduce | flops 256 | bytes 2048 | tf_op jit(solution)/shard_map/psum | solution.py:53
  921.5 5.5 collective-permute-start.5
  927.0 4.9 convolution_bitcast_fusion.1
  938.4 5.0 convolution_bitcast_fusion
  955.6 5.0 convolution_bitcast_fusion.2
  963.5 3.6 gather_fusion.9
  967.1 4.1 fusion.14
  971.3 3.6 gather_fusion.6
  981.9 5.1 bitcast_add_fusion
  990.3 347.1 %psum.31 = f32[256]{0:T(256)S(1)} all-reduce(f32[256]{0:T(256)S(1)} %multiply_reduce_fusion), channel_id=1, replica_groups=mesh['vert'=128,'qcol'=2] {'vert'}, use_global_device_ids=true, to_apply=%region_10.11 | all-reduce | flops 256 | bytes 2048 | tf_op jit(solution)/shard_map/psum | solution.py:75
  1337.5 4.6 multiply_subtract_fusion
  (70 shorter events, 77.5 us)
Async XLA Ops:
  7.2 107.9 %all-gather.2.cloned.1.call-start = ((), (), s32[]{:S(2)}) async-start(), calls=%async_computation | async-start | bytes 1056768 | tf_op jit(solution)/shard_map/all_gather | solution.py:42
  121.2 54.2 %collective-permute-start = (f32[2048,256]{1,0:T(8,128)S(1)}, f32[2048,256]{1,0:T(8,128)}, u32[]{:S(2)}, u32[]{:S(2)}) collective-permute-start(f32[2048,256]{1,0:T(8,128)S(1)} %fusion), channel_id=1, source_target_pairs={{0,2},{2,4},{4,6},{6,8},{8,10},{10,12},{12,14},{14,16},{16,18},{18... | collective-permute-start | bytes 6291464 | tf_op jit(solution)/shard_map/ppermute | solution.py:15
  122.6 56.4 %collective-permute-start.1 = (f32[2048,256]{1,0:T(8,128)S(1)}, f32[2048,256]{1,0:T(8,128)}, u32[]{:S(2)}, u32[]{:S(2)}) collective-permute-start(f32[2048,256]{1,0:T(8,128)S(1)} %fusion), channel_id=1, source_target_pairs={{2,0},{4,2},{6,4},{8,6},{10,8},{12,10},{14,12},{16,14},{18,16},{20... | collective-permute-start | bytes 6291464 | tf_op jit(solution)/shard_map/ppermute | solution.py:18
  139.5 74.9 %collective-permute-start.2 = (f32[16,128,256]{2,1,0:T(8,128)}, f32[16,128,256]{2,1,0:T(8,128)}, u32[]{:S(2)}, u32[]{:S(2)}) collective-permute-start(f32[16,128,256]{2,1,0:T(8,128)} %gather_fusion.4), channel_id=1, source_target_pairs={{0,254},{2,0},{4,2},{6,4},{8,6},{10,8},{12,10},{14,12},{16,14},{18... | collective-permute-start | bytes 6291464 | tf_op jit(solution)/shard_map/ppermute | solution.py:25
  151.6 63.5 %collective-permute-start.3 = (f32[16,128,256]{2,1,0:T(8,128)}, f32[16,128,256]{2,1,0:T(8,128)}, u32[]{:S(2)}, u32[]{:S(2)}) collective-permute-start(f32[16,128,256]{2,1,0:T(8,128)} %gather_fusion.5), channel_id=1, source_target_pairs={{0,2},{2,4},{4,6},{6,8},{8,10},{10,12},{12,14},{14,16},{16,18},{18... | collective-permute-start | bytes 6291464 | tf_op jit(solution)/shard_map/ppermute | solution.py:25
  182.7 32.5 %copy-start.4 = (f32[16,128,256]{2,1,0:T(8,128)S(1)}, f32[16,128,256]{2,1,0:T(8,128)}, u32[]{:S(2)}) copy-start(f32[16,128,256]{2,1,0:T(8,128)} %gather_fusion.3) | copy-start | bytes 6291460
  182.7 32.5 %copy-start.5 = (f32[16,256,128]{1,2,0:T(8,128)S(1)}, f32[16,256,128]{1,2,0:T(8,128)}, u32[]{:S(2)}) copy-start(f32[16,256,128]{1,2,0:T(8,128)} %fusion.17) | copy-start | bytes 6291460
  220.3 1.4 copy-start
  919.5 51.7 %collective-permute-start.4 = (f32[2048,256]{1,0:T(8,128)}, f32[2048,256]{1,0:T(8,128)}, u32[]{:S(2)}, u32[]{:S(2)}) collective-permute-start(f32[2048,256]{1,0:T(8,128)} %multiply_add_fusion.1), channel_id=1, source_target_pairs={{0,2},{2,4},{4,6},{6,8},{8,10},{10,12},{12,14},{14,16},{16,18},{18... | collective-permute-start | bytes 6291464 | tf_op jit(solution)/shard_map/ppermute | solution.py:15
  921.5 53.4 %collective-permute-start.5 = (f32[2048,256]{1,0:T(8,128)}, f32[2048,256]{1,0:T(8,128)}, u32[]{:S(2)}, u32[]{:S(2)}) collective-permute-start(f32[2048,256]{1,0:T(8,128)} %multiply_add_fusion.1), channel_id=1, source_target_pairs={{2,0},{4,2},{6,4},{8,6},{10,8},{12,10},{14,12},{16,14},{18,16},{20... | collective-permute-start | bytes 6291464 | tf_op jit(solution)/shard_map/ppermute | solution.py:18
  938.4 43.0 %collective-permute-start.6 = (f32[16,128,256]{2,1,0:T(8,128)}, f32[16,128,256]{2,1,0:T(8,128)}, u32[]{:S(2)}, u32[]{:S(2)}) collective-permute-start(f32[16,128,256]{2,1,0:T(8,128)} %gather_fusion.10), channel_id=1, source_target_pairs={{0,254},{2,0},{4,2},{6,4},{8,6},{10,8},{12,10},{14,12},{16,14},{18... | collective-permute-start | bytes 6291464 | tf_op jit(solution)/shard_map/ppermute | solution.py:25
  949.9 32.0 %collective-permute-start.7 = (f32[16,128,256]{2,1,0:T(8,128)}, f32[16,128,256]{2,1,0:T(8,128)}, u32[]{:S(2)}, u32[]{:S(2)}) collective-permute-start(f32[16,128,256]{2,1,0:T(8,128)} %gather_fusion.11), channel_id=1, source_target_pairs={{0,2},{2,4},{4,6},{6,8},{8,10},{10,12},{12,14},{14,16},{16,18},{18... | collective-permute-start | bytes 6291464 | tf_op jit(solution)/shard_map/ppermute | solution.py:25
  978.5 3.5 copy-start.2
  978.5 3.5 copy-start.3
  987.1 1.3 copy-start.1
Sparse Core Ops, SparseCore 0:
  11.4 103.6 all-gather.1
where the time goes:
time: 1350 us
  blocking collectives  1040 us (77%)
  waiting for transfers between devices  136 us (10%)
  local copies, waits for them, and re-layouts  63.5 us (5%)
  matrix products  58.4 us (4%)
  starting transfers between devices  19.1 us (1%)
  other arithmetic  17.7 us (1%)
  between operations  14.2 us (1%)
    psum x2, blocking collectives, squares(): return lax.psum(jnp.sum(values * values, axis=0), 'vert')  692 us
    psum x1, blocking collectives, body(): curve = lax.psum(jnp.sum(direction * image, axis=0), 'vert')  347 us
    all_gather x1, waiting for transfers between devices, body(): lax.all_gather(queries, 'vert', axis=1, tiled=True)  100 us
    ppermute x4, waiting for transfers between devices, shifted(): return lax.ppermute(x, axis, [(i, (i + by) % peers) for i in range(peers)])  30 us
    dot_general x6, matrix products, transposed(): jnp.einsum('rba,rbq->raq', blocks_slot, rows3, precision=lax.Precision.HI...  27.8 us
  transfers between devices with their start and end apart: 9, of which 5 were waited for; matrix products, arithmetic and copies ran while one was open for 8% of the time, Pallas kernels for 0%

commit v1 on v0

--- a/solution.py
+++ b/solution.py
@@ -72,7 +72,7 @@
         back = middle + shifted(toward_low, "vert", -1) + shifted(toward_high, "vert", 1)
         both = (forward + back).reshape(rows, qdev)
         image = direction - 0.99 * live * (0.5 * both)
-        curve = lax.psum(jnp.sum(direction * image, axis=0), "vert")
+        curve = jnp.sum(lax.all_gather(jnp.sum(direction * image, axis=0), "vert"), axis=0)
         alpha = norm_now / curve
         ranking = ranking + alpha[None, :] * direction
         residual = residual - alpha[None, :] * image

time: 1350 us -> 1690 us (1.25)
  blocking collectives: 1040 us -> 1380 us
    all_gather x0 -> x2, blocking collectives: none -> 688 us  [body(): lax.all_gather(jnp.sum(direction * image, axis=0), 'vert')]
    psum x1 -> x0, blocking collectives: 347 us -> none  [body(): curve = lax.psum(jnp.sum(direction * image, axis=0), 'vert')]
  transfers between devices with their start and end apart: 9 -> 9, of which waited for: 5 -> 5; matrix products, arithmetic and copies ran while one was open for 8% -> 6% of each run, Pallas kernels for 0% -> 0%
where the time goes in v1:
time: 1690 us; the launch traced here: 1680 us
  blocking collectives  1380 us (82%)
  waiting for transfers between devices  136 us (8%)
  local copies, waits for them, and re-layouts  62.3 us (4%)
  matrix products  58.4 us (3%)
  starting transfers between devices  19.1 us (1%)
  other arithmetic  18.7 us (1%)
    all_gather x2, blocking collectives, body(): lax.all_gather(jnp.sum(direction * image, axis=0), 'vert')  688 us
    psum x2, blocking collectives, squares(): return lax.psum(jnp.sum(values * values, axis=0), 'vert')  687 us
    all_gather x1, waiting for transfers between devices, body(): lax.all_gather(queries, 'vert', axis=1, tiled=True)  100 us
  transfers between devices with their start and end apart: 9, of which 5 were waited for; matrix products, arithmetic and copies ran while one was open for 6% of the time, Pallas kernels for 0%

profile of v1, /device:TPU:0, one launch (start us, length us, event | category | flops | bytes accessed | tf_op | source)
XLA Modules:
  0.0 1684.5 jit_solution(7018861464725111210)
XLA Ops:
  14.6 100.5 %all-gather.6.cloned.1.call-done = bf16[256,2048]{0,1:T(8,128)(2,1)} async-done(((bf16[256,16]{0,1:T(8,128)(2,1)}), bf16[256,2048]{0,1:T(8,128)(2,1)}) %all-gather.6.cloned.1.call-update) | async-done | bytes 1048592 | tf_op jit(solution)/shard_map/all_gather | solution.py:42
  115.1 6.1 fusion
  122.6 6.1 collective-permute-start.1
  128.7 4.3 convolution_bitcast_fusion.4
  140.9 4.3 convolution_bitcast_fusion.3
  153.1 4.3 convolution_bitcast_fusion.5
  165.9 4.1 fusion.17
  170.0 5.3 collective-permute-done
  175.4 3.6 gather_fusion
  179.0 3.7 gather_fusion.2
  185.7 28.8 %collective-permute-done.2 = f32[16,128,256]{2,1,0:T(8,128)} collective-permute-done((f32[16,128,256]{2,1,0:T(8,128)}, f32[16,128,256]{2,1,0:T(8,128)}, u32[]{:S(2)}, u32[]{:S(2)}) %collective-permute-start.2) | collective-permute-done | bytes 2097184 | tf_op jit(solution)/shard_map/ppermute | solution.py:25
  215.2 5.1 bitcast_add_fusion.1
  221.7 345.2 %all-gather.2 = f32[128,1,256]{2,1,0:T(1,128)S(1)} all-gather(f32[1,1,256]{2,1,0:T(1,128)S(1)} %bitcast.78), channel_id=2, replica_groups=mesh['vert'=128,'qcol'=2] {'vert'}, dimensions={0}, use_global_device_ids=true | all-gather | bytes 132096 | tf_op jit(solution)/shard_map/all_gather | solution.py:75
  566.8 342.2 %psum.14 = f32[256]{0:T(256)S(1)} all-reduce(f32[256]{0:T(256)S(1)} %get-tuple-element.9), channel_id=1, replica_groups=mesh['vert'=128,'qcol'=2] {'vert'}, use_global_device_ids=true, to_apply=%region_1.2 | all-reduce | flops 256 | bytes 2048 | tf_op jit(solution)/shard_map/psum | solution.py:53
  911.3 345.0 %psum.15 = f32[256]{0:T(256)S(1)} all-reduce(f32[256]{0:T(256)S(1)} %multiply_reduce_fusion.1), channel_id=1, replica_groups=mesh['vert'=128,'qcol'=2] {'vert'}, use_global_device_ids=true, to_apply=%region_8.9 | all-reduce | flops 256 | bytes 2048 | tf_op jit(solution)/shard_map/psum | solution.py:53
  1259.7 7.5 collective-permute-start.5
  1267.1 4.9 convolution_bitcast_fusion.1
  1278.6 5.0 convolution_bitcast_fusion
  1295.7 5.0 convolution_bitcast_fusion.2
  1303.6 3.6 gather_fusion.9
  1307.2 4.1 fusion.14
  1321.9 5.1 bitcast_add_fusion
  1329.8 343.2 %all-gather.3 = f32[128,1,256]{2,1,0:T(1,128)S(1)} all-gather(f32[1,1,256]{2,1,0:T(1,128)S(1)} %bitcast.77), channel_id=3, replica_groups=mesh['vert'=128,'qcol'=2] {'vert'}, dimensions={0}, use_global_device_ids=true | all-gather | bytes 132096 | tf_op jit(solution)/shard_map/all_gather | solution.py:75
  1673.1 4.6 multiply_subtract_fusion
  (73 shorter events, 78.7 us)
Async XLA Ops:
  7.2 107.9 %all-gather.6.cloned.1.call-start = ((), (), s32[]{:S(2)}) async-start(), calls=%async_computation | async-start | bytes 1056768 | tf_op jit(solution)/shard_map/all_gather | solution.py:42
  121.2 54.2 %collective-permute-start = (f32[2048,256]{1,0:T(8,128)S(1)}, f32[2048,256]{1,0:T(8,128)}, u32[]{:S(2)}, u32[]{:S(2)}) collective-permute-start(f32[2048,256]{1,0:T(8,128)S(1)} %fusion), channel_id=1, source_target_pairs={{0,2},{2,4},{4,6},{6,8},{8,10},{10,12},{12,14},{14,16},{16,18},{18... | collective-permute-start | bytes 6291464 | tf_op jit(solution)/shard_map/ppermute | solution.py:15
  122.6 56.4 %collective-permute-start.1 = (f32[2048,256]{1,0:T(8,128)S(1)}, f32[2048,256]{1,0:T(8,128)}, u32[]{:S(2)}, u32[]{:S(2)}) collective-permute-start(f32[2048,256]{1,0:T(8,128)S(1)} %fusion), channel_id=1, source_target_pairs={{2,0},{4,2},{6,4},{8,6},{10,8},{12,10},{14,12},{16,14},{18,16},{20... | collective-permute-start | bytes 6291464 | tf_op jit(solution)/shard_map/ppermute | solution.py:18
  139.5 74.9 %collective-permute-start.2 = (f32[16,128,256]{2,1,0:T(8,128)}, f32[16,128,256]{2,1,0:T(8,128)}, u32[]{:S(2)}, u32[]{:S(2)}) collective-permute-start(f32[16,128,256]{2,1,0:T(8,128)} %gather_fusion.4), channel_id=1, source_target_pairs={{0,254},{2,0},{4,2},{6,4},{8,6},{10,8},{12,10},{14,12},{16,14},{18... | collective-permute-start | bytes 6291464 | tf_op jit(solution)/shard_map/ppermute | solution.py:25
  151.6 63.5 %collective-permute-start.3 = (f32[16,128,256]{2,1,0:T(8,128)}, f32[16,128,256]{2,1,0:T(8,128)}, u32[]{:S(2)}, u32[]{:S(2)}) collective-permute-start(f32[16,128,256]{2,1,0:T(8,128)} %gather_fusion.5), channel_id=1, source_target_pairs={{0,2},{2,4},{4,6},{6,8},{8,10},{10,12},{12,14},{14,16},{16,18},{18... | collective-permute-start | bytes 6291464 | tf_op jit(solution)/shard_map/ppermute | solution.py:25
  182.7 32.5 %copy-start.4 = (f32[16,128,256]{2,1,0:T(8,128)S(1)}, f32[16,128,256]{2,1,0:T(8,128)}, u32[]{:S(2)}) copy-start(f32[16,128,256]{2,1,0:T(8,128)} %gather_fusion.3) | copy-start | bytes 6291460
  182.7 32.5 %copy-start.5 = (f32[16,256,128]{1,2,0:T(8,128)S(1)}, f32[16,256,128]{1,2,0:T(8,128)}, u32[]{:S(2)}) copy-start(f32[16,256,128]{1,2,0:T(8,128)} %fusion.17) | copy-start | bytes 6291460
  220.3 1.4 copy-start
  1259.7 51.7 %collective-permute-start.4 = (f32[2048,256]{1,0:T(8,128)}, f32[2048,256]{1,0:T(8,128)}, u32[]{:S(2)}, u32[]{:S(2)}) collective-permute-start(f32[2048,256]{1,0:T(8,128)} %multiply_add_fusion.1), channel_id=1, source_target_pairs={{0,2},{2,4},{4,6},{6,8},{8,10},{10,12},{12,14},{14,16},{16,18},{18... | collective-permute-start | bytes 6291464 | tf_op jit(solution)/shard_map/ppermute | solution.py:15
  1259.7 55.3 %collective-permute-start.5 = (f32[2048,256]{1,0:T(8,128)}, f32[2048,256]{1,0:T(8,128)}, u32[]{:S(2)}, u32[]{:S(2)}) collective-permute-start(f32[2048,256]{1,0:T(8,128)} %multiply_add_fusion.1), channel_id=1, source_target_pairs={{2,0},{4,2},{6,4},{8,6},{10,8},{12,10},{14,12},{16,14},{18,16},{20... | collective-permute-start | bytes 6291464 | tf_op jit(solution)/shard_map/ppermute | solution.py:18
  1278.6 43.0 %collective-permute-start.6 = (f32[16,128,256]{2,1,0:T(8,128)}, f32[16,128,256]{2,1,0:T(8,128)}, u32[]{:S(2)}, u32[]{:S(2)}) collective-permute-start(f32[16,128,256]{2,1,0:T(8,128)} %gather_fusion.10), channel_id=1, source_target_pairs={{0,254},{2,0},{4,2},{6,4},{8,6},{10,8},{12,10},{14,12},{16,14},{18... | collective-permute-start | bytes 6291464 | tf_op jit(solution)/shard_map/ppermute | solution.py:25
  1290.1 31.8 %collective-permute-start.7 = (f32[16,128,256]{2,1,0:T(8,128)}, f32[16,128,256]{2,1,0:T(8,128)}, u32[]{:S(2)}, u32[]{:S(2)}) collective-permute-start(f32[16,128,256]{2,1,0:T(8,128)} %gather_fusion.11), channel_id=1, source_target_pairs={{0,2},{2,4},{4,6},{6,8},{8,10},{10,12},{12,14},{14,16},{16,18},{18... | collective-permute-start | bytes 6291464 | tf_op jit(solution)/shard_map/ppermute | solution.py:25
  1318.6 3.3 copy-start.2
  1318.6 3.3 copy-start.3
  1327.0 2.7 copy-start.1
Sparse Core Ops, SparseCore 0:
  11.4 103.6 all-gather.5
